TPU v7x, 128 devices: a whole 4x4x4 slice. The times are simulated.
128 devices in a mesh: row: 8 (over y_lo, z), col: 16 (over x, y_hi, core).
Axes of the slice: x: 4, y: 4 (y_hi: 2, y_lo: 2; y = y_hi * 2 + y_lo), z: 4, core: 2. Of those that a mesh axis runs over, the one named last changes fastest.
Arguments:
- pair: float32 [512, 1024, 128], P('row', 'col'), may hold values from -6 to 6
- right_proj: bfloat16 [64, 1024, 1024], P(None, 'row', 'col'), may hold values from -3 to 3
- w_left_gate: bfloat16 [128, 64], replicated, may hold values from -0.5 to 0.5
- w_left: bfloat16 [128, 64], replicated, may hold values from -0.5 to 0.5
- w_gate: bfloat16 [128, 128], replicated, may hold values from -0.5 to 0.5
- out_gain: float32 [64], replicated, may hold values from 0.1 to 1.9
- w_out: bfloat16 [64, 128], replicated, may hold values from -0.75 to 0.75
- cotangent: float32 [512, 1024, 128], P('row', 'col'), may hold values from -6 to 6
Outputs:
- update: float32 [512, 1024, 128], P('row', 'col')
- grad_pair: float32 [512, 1024, 128], P('row', 'col')
- grad_right: bfloat16 [64, 1024, 1024], P(None, 'row', 'col')
All inputs are finite; a program needn't handle non-finite values.
Results may differ from a plain program's by a relative error of at most 0.02.
Values may be sent and summed in bfloat16 or wider, within the bound.
A program may use at most 192 MiB of HBM per device.

v0:
```python
import jax
import jax.numpy as jnp
from jax import lax
from jax.sharding import PartitionSpec as P

EPS = 1e-05


def normalize(values):
    centred = values - jnp.mean(values, -1, keepdims=True)
    inv_std = lax.rsqrt(jnp.mean(centred * centred, -1, keepdims=True) + EPS)
    return (centred * inv_std, inv_std)


def norm_back(grad, normed, inv_std):
    return inv_std * (
        grad
        - jnp.mean(grad, -1, keepdims=True)
        - normed * jnp.mean(grad * normed, -1, keepdims=True)
    )


def shards(pair, right_proj, w_left_gate, w_left, w_gate, out_gain, w_out, cotangent):
    normed, inv_in = normalize(pair)
    normed_low = normed.astype(jnp.bfloat16)
    left_logit = jnp.dot(normed_low, w_left_gate, preferred_element_type=jnp.float32)
    left_value = jnp.dot(normed_low, w_left, preferred_element_type=jnp.float32)
    left_sig = jax.nn.sigmoid(left_logit)
    left_heads = jnp.transpose((left_sig * left_value).astype(jnp.bfloat16), (2, 0, 1))
    left_full = lax.all_gather(left_heads, "col", axis=2, tiled=True)
    right_full = lax.all_gather(right_proj, "row", axis=1, tiled=True)
    triangle = jnp.einsum("hik,hkj->ijh", left_full, right_full, preferred_element_type=jnp.float32)
    tri_hat, inv_out = normalize(triangle)
    tri_low = (tri_hat * out_gain).astype(jnp.bfloat16)
    linear = jnp.dot(tri_low, w_out, preferred_element_type=jnp.float32)
    gate = jax.nn.sigmoid(jnp.dot(normed_low, w_gate, preferred_element_type=jnp.float32))
    update = gate * linear
    d_linear = cotangent * gate
    d_gate = cotangent * linear * gate * (1.0 - gate)
    d_scaled = (
        jnp.dot(d_linear.astype(jnp.bfloat16), w_out.T, preferred_element_type=jnp.float32)
        * out_gain
    )
    d_tri = norm_back(d_scaled, tri_hat, inv_out).astype(jnp.bfloat16)
    grad_heads = jnp.transpose(d_tri, (2, 0, 1))
    d_left = lax.psum_scatter(
        jnp.einsum(
            "hij,hkj->kih", grad_heads, right_full, preferred_element_type=jnp.float32
        ).astype(jnp.bfloat16),
        "col",
        scatter_dimension=0,
        tiled=True,
    ).astype(jnp.float32)
    d_left = jnp.transpose(d_left, (1, 0, 2))
    summed = lax.psum_scatter(
        jnp.einsum(
            "hik,hij->khj", left_full, grad_heads, preferred_element_type=jnp.float32
        ).astype(jnp.bfloat16),
        "row",
        scatter_dimension=0,
        tiled=True,
    ).astype(jnp.float32)
    grad_right = jnp.transpose(summed, (1, 0, 2)).astype(jnp.bfloat16)
    d_value = d_left * left_sig
    d_logit = d_left * left_value * left_sig * (1.0 - left_sig)
    stacked = jnp.concatenate([d_value, d_logit, d_gate], -1).astype(jnp.bfloat16)
    weights = jnp.concatenate([w_left, w_left_gate, w_gate], 1)
    d_normed = jnp.dot(stacked, weights.T, preferred_element_type=jnp.float32)
    grad_pair = norm_back(d_normed, normed, inv_in)
    return (update, grad_pair, grad_right)


def solution(mesh):
    in_specs = (
        P("row", "col", None),
        P(None, "row", "col"),
        P(),
        P(),
        P(),
        P(),
        P(),
        P("row", "col", None),
    )
    out_specs = (P("row", "col", None), P("row", "col", None), P(None, "row", "col"))
    return jax.shard_map(shards, mesh=mesh, in_specs=in_specs, out_specs=out_specs, check_vma=False)
```

profile of v0, /device:TPU:1, one launch (start us, length us, event | category | flops | bytes accessed | tf_op | source)
XLA Modules:
  0.0 503.9 jit_solution(12940673398521791774)
XLA Ops:
  7.2 2.3 reduce_sum.72
  15.6 1.4 fusion.16
  17.0 3.0 copy.37
  22.9 2.5 fusion.15
  25.3 108.7 %all-gather.3.cloned.1.call-done = bf16[64,64,1024]{1,0,2:T(8,128)(2,1)} async-done(((bf16[64,64,64]{1,0,2:T(8,128)(2,1)}), bf16[64,64,1024]{1,0,2:T(8,128)(2,1)}) %all-gather.3.cloned.1.call-update) | async-done | bytes 8388624 | tf_op jit(solution)/shard_map/all_gather | solution.py:30
  134.0 18.4 %copy.38 = bf16[64,64,1024]{2,1,0:T(8,128)(2,1)} copy(bf16[64,64,1024]{1,0,2:T(8,128)(2,1)} %all-gather.3.cloned.1.call-done) | data formatting | bytes 16777216 | tf_op jit(solution)/shard_map/all_gather | solution.py:30
  152.4 76.0 %all-gather.5.cloned.1.call-done = bf16[64,1024,64]{1,2,0:T(8,128)(2,1)} async-done(((bf16[64,128,64]{1,2,0:T(8,128)(2,1)}), bf16[64,1024,64]{1,2,0:T(8,128)(2,1)}) %all-gather.5.cloned.1.call-update) | async-done | bytes 8388624 | tf_op jit(solution)/shard_map/all_gather | solution.py:31
  228.3 8.1 %bitcast_reduce_fusion = (f32[64,64]{1,0:T(8,128)S(1)}, f32[64,64,64]{2,1,0:T(8,128)S(1)}) fusion(bf16[64,64,1024]{2,1,0:T(8,128)(2,1)} %copy.38, bf16[64,1024,64]{1,2,0:T(8,128)(2,1)} %all-gather.5.cloned.1.call-done), kind=kOutput, calls=%fused_computation.18 | convolution fusion | flops 537128960 | bytes 17842176 | tf_op jit(solution)/shard_map/hik,hkj->ijh/dot_general | solution.py:32
  238.0 2.7 fusion.14
  240.7 1.5 fusion.11
  242.3 5.6 %convert_bitcast_fusion = bf16[1024,64,64]{0,1,2:T(8,128)(2,1)} fusion(bf16[64,64,64]{2,1,0:T(8,128)(2,1)S(1)} %fusion.11, bf16[64,1024,64]{1,2,0:T(8,128)(2,1)S(1)} %copy-done.2), kind=kOutput, calls=%fused_computation | convolution fusion | flops 541065216 | bytes 17301504 | tf_op jit(solution)/shard_map/hij,hkj->kih/dot_general | solution.py:47
  247.8 24.0 %copy.47 = bf16[1024,64,64]{1,2,0:T(8,128)(2,1)} copy(bf16[1024,64,64]{0,1,2:T(8,128)(2,1)} %convert_bitcast_fusion) | data formatting | bytes 16777216
  271.9 22.6 %reshape.52 = bf16[1024,4096]{1,0:T(8,128)(2,1)} reshape(bf16[1024,64,64]{2,1,0:T(8,128)(2,1)} %bitcast.72) | data formatting | bytes 16777216
  294.7 9.0 %convolution_convert_fusion = bf16[64,64,1024]{2,1,0:T(8,128)(2,1)} fusion(bf16[64,64,64]{2,1,0:T(8,128)(2,1)S(1)} %fusion.11, bf16[64,64,1024]{2,1,0:T(8,128)(2,1)} %copy.38), kind=kOutput, calls=%fused_computation.1 | convolution fusion | flops 541065216 | bytes 17301504 | tf_op jit(solution)/shard_map/hik,hij->khj/dot_general | solution.py:56
  303.7 11.4 %copy.52 = bf16[1024,4096]{1,0:T(8,128)(2,1)} copy(bf16[1024,4096]{0,1:T(8,128)(2,1)} %bitcast.73) | data formatting | bytes 16777216
  316.4 5.4 %multiply_convert_fusion.1 = (bf16[64,64,128]{2,1,0:T(8,128)(2,1)}, f32[64,64,128]{2,1,0:T(8,128)}) fusion(f32[64,64,128]{2,1,0:T(8,128)} %copy-done.7, f32[64,64,128]{2,1,0:T(8,128)} %param.15, bf16[64,128]{1,0:T(8,128)(2,1)S(1)} %copy-done, bf16[64,64,64]{1,0,2:T(8,128)(2,1)S(1)} %copy-done.8), kind=kOutput, calls=%fused_computation.23 | convolution fusion | flops 70254592 | bytes 7880704 | tf_op jit(solution)/shard_map/dot_general | solution.py:35
  321.8 77.9 %reduce-scatter.7.cloned.1.call-done = bf16[64,4096]{1,0:T(8,128)(2,1)} async-done(((bf16[1024,4096]{1,0:T(8,128)(2,1)}), bf16[64,4096]{1,0:T(8,128)(2,1)}) %reduce-scatter.7.cloned.1.call-update) | async-done | bytes 524304
  399.8 2.7 reshape.53
  402.5 2.6 copy.41
  405.1 3.0 fusion.6
  408.2 3.1 fusion.30
  411.3 3.4 subtract_multiply_fusion
  414.7 80.4 %reduce-scatter.9.cloned.1.call-done = bf16[128,4096]{1,0:T(8,128)(2,1)} async-done(((bf16[1024,4096]{1,0:T(8,128)(2,1)}), bf16[128,4096]{1,0:T(8,128)(2,1)}) %reduce-scatter.9.cloned.1.call-update) | async-done | bytes 1048592
  495.1 2.3 copy.53
  (51 shorter events, 12.0 us)
Async XLA Ops:
  7.2 15.7 %copy-start = (bf16[64,128]{1,0:T(8,128)(2,1)S(1)}, bf16[64,128]{1,0:T(8,128)(2,1)}, u32[]{:S(2)}) copy-start(bf16[64,128]{1,0:T(8,128)(2,1)} %param.14) | copy-start | bytes 49156
  7.2 2.4 copy-start.1
  7.2 126.8 %all-gather.3.cloned.1.call-start = ((), (), s32[]{:S(2)}) async-start(), calls=%async_computation.2 | async-start | bytes 17825792 | tf_op jit(solution)/shard_map/all_gather | solution.py:30
  10.9 1.3 copy-start.10
  12.2 0.7 copy-start.11
  12.9 1.3 copy-start.3
  14.3 1.3 copy-start.5
  17.0 3.8 copy-start.13
  20.0 208.3 %all-gather.5.cloned.1.call-start = ((), (), s32[]{:S(2)}) async-start(), calls=%async_computation.3 | async-start | bytes 9437184 | tf_op jit(solution)/shard_map/all_gather | solution.py:31
  20.8 379.0 %reduce-scatter.7.cloned.1.call-start = ((), (), s32[]{:S(2)}) async-start(), calls=%async_computation.4 | async-start | bytes 8912896
  20.8 2.0 copy-start.6
  21.5 1.3 copy-start.7
  236.4 1.6 copy-start.4
  236.5 1.6 copy-start.12
  238.0 4.2 copy-start.2
  294.4 200.6 %reduce-scatter.9.cloned.1.call-start = ((), (), s32[]{:S(2)}) async-start(), calls=%async_computation.5 | async-start | bytes 9437184
  315.1 1.3 copy-start.8
  405.1 3.0 copy-start.9
Sparse Core Ops, SparseCore 0:
  20.1 113.8 all-gather.2
  135.6 92.7 all-gather.4
  294.6 105.1 reduce-scatter.6
  402.0 93.0 reduce-scatter.8
where the time goes:
time: 506 us; the launch traced here: 504 us
  waiting for transfers between devices  344 us (68%)
  local copies, waits for them, and re-layouts  93 us (18%)
  matrix products  35.4 us (7%)
  other arithmetic  17.4 us (3%)
  between operations  14 us (3%)
    unnamed x6, waiting for transfers between devices  159 us
    all_gather x1, waiting for transfers between devices, shards(): left_full = lax.all_gather(left_heads, 'col', axis=2, tiled=True)  109 us
    all_gather x1, waiting for transfers between devices, shards(): right_full = lax.all_gather(right_proj, 'row', axis=1, tiled=True)  76 us
    unnamed x35, local copies, waits for them, and re-layouts  69.1 us
    all_gather x1, local copies, waits for them, and re-layouts, shards(): left_full = lax.all_gather(left_heads, 'col', axis=2, tiled=True)  18.4 us
  transfers between devices with their start and end apart: 4, of which 4 were waited for; matrix products, arithmetic and copies ran while one was open for 12% of the time, Pallas kernels for 0%

commit v1 on v0

v1 whole, which is shorter than its diff:
```python
import functools

import jax
import jax.numpy as jnp
from jax import lax
from jax.experimental import pallas as pl
from jax.experimental.pallas import tpu as pltpu
from jax.sharding import PartitionSpec as P

EPS = 1e-05
F32 = jnp.float32
BF16 = jnp.bfloat16
MESH = pl.DeviceIdType.MESH

CH = 128
HID = 64
SIDE = 64
ROW = 8
COLC = 8
HALF = SIDE // 2
KB = 128
LANES = 128
PEERS = ROW * COLC


def dot(a, b, da, db):
    return lax.dot_general(a, b, (((da,), (db,)), ((), ())), preferred_element_type=F32)


def swap(a, b):
    left = lax.broadcasted_iota(jnp.int32, a.shape, a.ndim - 1) < LANES // 2
    ra = pltpu.roll(a, LANES // 2, a.ndim - 1)
    rb = pltpu.roll(b, LANES // 2, b.ndim - 1)
    return jnp.where(left, a, rb), jnp.where(left, ra, b)


def kernel(
    pair_hbm, right_hbm, wlg_ref, wl_ref, wg_ref, gain_ref, wo_ref, cot_hbm,
    upd_hbm, gp_hbm, gr_hbm,
    xn, cot, inv, gate, sig, val, dgate, upd,
    stage, send8, lb, lfull, rt, tm, tr, dtr, dtfull, grs, dlk, dlx, dly, dls, dlr, wcat, gcol,
    io_sem, send_sem, recv_sem,
):
    row, col = lax.axis_index("row"), lax.axis_index("col")
    core = lax.rem(col, 2)
    colc = col // 2
    me = row * COLC + colc
    sibling = (row, colc * 2 + (1 - core))

    def peer(off):
        prow = lax.rem(row + off // COLC, ROW)
        pcol = lax.rem(colc + lax.rem(off, COLC), COLC)
        return prow * COLC + pcol, (prow, pcol * 2 + core)

    load_pair = pltpu.make_async_copy(pair_hbm, xn, io_sem.at[0])
    load_pair.start()
    load_cot = pltpu.make_async_copy(cot_hbm, cot, io_sem.at[1])
    load_cot.start()

    barrier = pltpu.get_barrier_semaphore()

    def greet(off, _):
        pl.semaphore_signal(barrier, inc=1, device_id=peer(off)[1], device_id_type=MESH)
        return 0

    lax.fori_loop(1, PEERS, greet, 0)
    pl.semaphore_signal(barrier, inc=1, device_id=sibling, device_id_type=MESH)
    pl.semaphore_wait(barrier, PEERS)

    def exchange(src_of, dst, phase):
        pltpu.make_async_copy(src_of(me), dst, recv_sem.at[phase]).start()

        def one(off, _):
            q, device = peer(off)
            pltpu.make_async_remote_copy(
                src_ref=src_of(q),
                dst_ref=dst,
                send_sem=send_sem.at[phase],
                recv_sem=recv_sem.at[phase],
                device_id=device,
                device_id_type=MESH,
            ).start()
            return 0

        lax.fori_loop(1, PEERS, one, 0)

    def arrived(buf, phase):
        pltpu.make_async_copy(buf, buf, recv_sem.at[phase]).wait()

    def sent(buf, phase):
        part = buf.at[pl.ds(0, PEERS - 1)]
        pltpu.make_async_copy(part, part, send_sem.at[phase]).wait()

    exchange(lambda q: right_hbm.at[q], rt.at[row * COLC + colc], 0)

    wcat[:HID] = wl_ref[...]
    wcat[HID:] = wlg_ref[...]
    eye = lax.broadcasted_iota(jnp.int32, (HID, HID), 0) == lax.broadcasted_iota(jnp.int32, (HID, HID), 1)
    column = jnp.sum(jnp.where(eye, gain_ref[...], 0.0), axis=1, keepdims=True)
    gcol[...] = jnp.broadcast_to(column, (HID, LANES))

    load_pair.wait()

    def left_step(s, _):
        x = jnp.concatenate([xn[s], xn[s + HALF]], axis=0)
        centred = x - jnp.mean(x, -1, keepdims=True)
        inv_std = lax.rsqrt(jnp.mean(centred * centred, -1, keepdims=True) + EPS)
        normed = centred * inv_std
        xn[s] = normed[:SIDE]
        xn[s + HALF] = normed[SIDE:]
        inv[s] = jnp.broadcast_to(inv_std, (LANES, CH))
        low = normed.astype(BF16)
        both = dot(wcat[...], low, 1, 1)
        value = both[:HID]
        left_sig = jax.nn.sigmoid(both[HID:])
        val[s] = value
        sig[s] = left_sig
        stage[pl.ds(s, HID, stride=HALF), :] = left_sig * value
        return 0

    lax.fori_loop(0, HALF, left_step, 0, unroll=2)

    def pack(h, _):
        send8[h] = stage[pl.ds(h * HALF, HALF), :].astype(BF16)
        return 0

    lax.fori_loop(0, HID, pack, 0, unroll=4)
    exchange(lambda q: send8.at[q], lb.at[core, me], 1)

    def gate_step(s, _):
        low = jnp.concatenate([xn[s], xn[s + HALF]], axis=0).astype(BF16)
        gate[s] = jax.nn.sigmoid(dot(low, wg_ref[...], 1, 0))
        return 0

    lax.fori_loop(0, HALF, gate_step, 0, unroll=2)

    arrived(lb.at[core], 1)
    swap_left = pltpu.make_async_remote_copy(
        src_ref=lb.at[core],
        dst_ref=lb.at[core],
        send_sem=send_sem.at[2],
        recv_sem=recv_sem.at[2],
        device_id=sibling,
        device_id_type=MESH,
    )
    swap_left.start()
    arrived(lb.at[1 - core], 2)

    def unpack_left(q, _):
        r, c = q // COLC, lax.rem(q, COLC)
        top, bottom = swap(lb[0, q].astype(F32), lb[1, q].astype(F32))
        block = jnp.concatenate([top, bottom], axis=0).astype(BF16)
        lfull[c, pl.ds(pl.multiple_of(r * SIDE, SIDE), SIDE), :] = block
        return 0

    lax.fori_loop(0, PEERS, unpack_left, 0, unroll=2)

    def k_left(lo, rows=slice(None)):
        return jnp.concatenate([lfull[lo, rows], lfull[lo + 1, rows]], axis=1)

    def k_right(lo):
        a = jnp.concatenate([rt[lo * COLC + c] for c in range(COLC)], axis=0)
        b = jnp.concatenate([rt[(lo + 1) * COLC + c] for c in range(COLC)], axis=0)
        return jnp.concatenate([a, b], axis=1)

    arrived(rt, 0)

    TI = 256

    def triangle_step(t, _):
        rows = pl.ds(pl.multiple_of(t * TI, TI), TI)
        total = dot(k_left(0, rows), k_right(0), 1, 1)
        for lo in range(2, ROW, 2):
            total += dot(k_left(lo, rows), k_right(lo), 1, 1)
        for rr in range(TI // SIDE):
            for p in range(COLC // 2):
                lanes = slice(p * LANES, (p + 1) * LANES)
                a, b = swap(
                    total[rr * SIDE : rr * SIDE + HALF, lanes],
                    total[rr * SIDE + HALF : (rr + 1) * SIDE, lanes],
                )
                at = (t * (TI // SIDE) + rr) * COLC + 2 * p
                tm[at] = a.astype(BF16)
                tm[at + 1] = b.astype(BF16)
        return 0

    lax.fori_loop(0, ROW * SIDE // TI, triangle_step, 0)
    exchange(lambda q: tm.at[q], tr.at[me], 3)

    sent(send8, 1)
    arrived(tr, 3)

    def widen(buf):
        def one(h, _):
            stage[pl.ds(pl.multiple_of(h * HALF, HALF), HALF), :] = buf[h].astype(F32)
            return 0

        lax.fori_loop(0, HID, one, 0, unroll=4)

    widen(tr)
    load_cot.wait()

    def middle_step(s, _):
        tri = stage[pl.ds(s, HID, stride=HALF), :]
        centred = tri - jnp.mean(tri, 0, keepdims=True)
        inv_out = lax.rsqrt(jnp.mean(centred * centred, 0, keepdims=True) + EPS)
        hat = centred * inv_out
        gain = gcol[...]
        linear = dot((hat * gain).astype(BF16), wo_ref[...], 0, 0)
        g = gate[s]
        update = g * linear
        upd[s] = update[:SIDE]
        upd[s + HALF] = update[SIDE:]
        ct = jnp.concatenate([cot[s], cot[s + HALF]], axis=0)
        d_linear = ct * g
        dgate[s] = (ct * linear * g * (1.0 - g)).astype(BF16)
        d_scaled = dot(wo_ref[...], d_linear.astype(BF16), 1, 1) * gain
        d_tri = inv_out * (
            d_scaled
            - jnp.mean(d_scaled, 0, keepdims=True)
            - hat * jnp.mean(d_scaled * hat, 0, keepdims=True)
        )
        stage[pl.ds(s, HID, stride=HALF), :] = d_tri
        return 0

    lax.fori_loop(0, HALF, middle_step, 0, unroll=2)
    lax.fori_loop(0, HID, pack, 0, unroll=4)
    exchange(lambda q: send8.at[q], dtr.at[me], 4)
    store_upd = pltpu.make_async_copy(upd, upd_hbm, io_sem.at[2])
    store_upd.start()

    arrived(dtr, 4)

    def unpack_tri(n, _):
        r, p = n // (COLC // 2), lax.rem(n, COLC // 2)
        at = r * COLC + 2 * p
        top, bottom = swap(dtr[at].astype(F32), dtr[at + 1].astype(F32))
        block = jnp.concatenate([top, bottom], axis=0).astype(BF16)
        dtfull[p, pl.ds(pl.multiple_of(r * SIDE, SIDE), SIDE), :] = block
        return 0

    lax.fori_loop(0, PEERS // 2, unpack_tri, 0, unroll=2)
    d_tri_all = jnp.concatenate([dtfull[p] for p in range(COLC // 2)], axis=1)

    for lo in range(0, ROW, 2):
        part = dot(d_tri_all, k_right(lo), 1, 0)
        for c in range(2):
            for r in range(ROW):
                lanes = slice(c * LANES, (c + 1) * LANES)
                for_0, for_1 = swap(
                    part[r * SIDE : r * SIDE + HALF, lanes],
                    part[r * SIDE + HALF : (r + 1) * SIDE, lanes],
                )
                at = r * COLC + lo + c
                first = core == 0
                dlk[at] = jnp.where(first, for_0, for_1)
                dlx[at] = jnp.where(first, for_1, for_0).astype(BF16)
    swap_grad = pltpu.make_async_remote_copy(
        src_ref=dlx,
        dst_ref=dly,
        send_sem=send_sem.at[5],
        recv_sem=recv_sem.at[5],
        device_id=sibling,
        device_id_type=MESH,
    )
    swap_grad.start()

    for lo in range(0, COLC, 2):
        part = dot(d_tri_all, k_left(lo), 0, 0).astype(BF16)
        for c in range(2):
            for cc in range(COLC):
                grs[(lo + c) * COLC + cc] = part[cc * SIDE : (cc + 1) * SIDE, c * LANES : (c + 1) * LANES]

    swap_grad.wait_recv()

    def add_halves(q, _):
        dls[q] = (dlk[q] + dly[q].astype(F32)).astype(BF16)
        return 0

    lax.fori_loop(0, PEERS, add_halves, 0, unroll=4)
    exchange(lambda q: dls.at[q], dlr.at[me], 6)
    exchange(lambda q: grs.at[q], gr_hbm.at[me], 7)

    arrived(dlr, 6)
    widen(dlr)

    def final_step(s, _):
        d_left = stage[pl.ds(s, HID, stride=HALF), :]
        left_sig, value = sig[s], val[s]
        d_value = d_left * left_sig
        d_logit = d_left * value * left_sig * (1.0 - left_sig)
        stacked = jnp.concatenate([d_value, d_logit], axis=0).astype(BF16)
        grad = dot(stacked, wcat[...], 0, 0) + dot(dgate[s], wg_ref[...], 1, 1)
        normed = jnp.concatenate([xn[s], xn[s + HALF]], axis=0)
        out = inv[s] * (
            grad
            - jnp.mean(grad, -1, keepdims=True)
            - normed * jnp.mean(grad * normed, -1, keepdims=True)
        )
        xn[s] = out[:SIDE]
        xn[s + HALF] = out[SIDE:]
        return 0

    lax.fori_loop(0, HALF, final_step, 0, unroll=2)
    store_gp = pltpu.make_async_copy(xn, gp_hbm, io_sem.at[3])
    store_gp.start()

    sent(right_hbm, 0)
    swap_left.wait_send()
    sent(tm, 3)
    sent(send8, 4)
    swap_grad.wait_send()
    sent(dls, 6)
    sent(grs, 7)
    store_upd.wait()
    arrived(gr_hbm, 7)
    store_gp.wait()


def shards(pair, right_proj, w_left_gate, w_left, w_gate, out_gain, w_out, cotangent):
    any_spec = pl.BlockSpec(memory_space=pl.ANY)
    vmem = pl.BlockSpec(memory_space=pltpu.VMEM)
    cells = (SIDE, SIDE, CH)
    block8 = (PEERS, HALF, LANES)
    block16 = (PEERS, SIDE, KB)
    per_step = (HALF, LANES, CH)
    heads = (HALF, HID, LANES)
    scratch = [
        (cells, F32), (cells, F32), (per_step, F32), (per_step, F32), (heads, F32), (heads, F32),
        (per_step, BF16), (cells, F32),
        ((HID * HALF, LANES), F32),
        (block8, BF16),
        ((2,) + block8, BF16),
        ((COLC, ROW * SIDE, LANES), BF16),
        (block16, BF16),
        (block8, BF16),
        (block8, BF16),
        (block8, BF16),
        ((COLC // 2, ROW * SIDE, LANES), BF16),
        (block16, BF16),
        (block8, F32),
        (block8, BF16), (block8, BF16), (block8, BF16), (block8, BF16),
        ((2 * HID, CH), BF16),
        ((HID, LANES), F32),
    ]
    update, grad_pair, grad_right = pl.pallas_call(
        kernel,
        out_shape=(
            jax.ShapeDtypeStruct(cells, F32),
            jax.ShapeDtypeStruct(cells, F32),
            jax.ShapeDtypeStruct((HID, SIDE, KB), BF16),
        ),
        in_specs=[any_spec, any_spec, vmem, vmem, vmem, vmem, vmem, any_spec],
        out_specs=(any_spec, any_spec, any_spec),
        scratch_shapes=[pltpu.VMEM(shape, dtype) for shape, dtype in scratch]
        + [
            pltpu.SemaphoreType.DMA((4,)),
            pltpu.SemaphoreType.DMA((8,)),
            pltpu.SemaphoreType.DMA((8,)),
        ],
        compiler_params=pltpu.CompilerParams(
            collective_id=0, has_side_effects=True, vmem_limit_bytes=56 * 1024 * 1024
        ),
    )(
        pair,
        jnp.transpose(right_proj, (0, 2, 1)),
        w_left_gate.T,
        w_left.T,
        w_gate,
        out_gain.reshape(1, HID),
        w_out,
        cotangent,
    )
    return update, grad_pair, jnp.transpose(grad_right, (0, 2, 1))


def solution(mesh):
    in_specs = (
        P("row", "col", None),
        P(None, "row", "col"),
        P(),
        P(),
        P(),
        P(),
        P(),
        P("row", "col", None),
    )
    out_specs = (P("row", "col", None), P("row", "col", None), P(None, "row", "col"))
    return jax.shard_map(shards, mesh=mesh, in_specs=in_specs, out_specs=out_specs, check_vma=False)
```

time: 506 us -> 96.5 us (0.19)
  waiting for transfers between devices: 344 us -> 0 us
  Pallas kernels: 0 us -> 89.4 us
  local copies, waits for them, and re-layouts: 93 us -> 6.24 us
  matrix products: 35.4 us -> 0 us
  other arithmetic: 17.4 us -> 0 us
  between operations: 14 us -> 0.65 us
    all_gather x2 -> x0, waiting for transfers between devices: 185 us -> none  [the longest x1 109 us: shards(): left_full = lax.all_gather(left_heads, 'col', axis=2, tiled=True)]
    unnamed x6 -> x0, waiting for transfers between devices: 159 us -> none
    pallas_call x0 -> x1, Pallas kernels: none -> 89.4 us  [shards(): pl.pallas_call(kernel, out_shape=(jax.ShapeDtypeStruct(cells, F32), jax.S...]
    unnamed x35 -> x7, local copies, waits for them, and re-layouts: 69.1 us -> 6.24 us
    dot_general x9 -> x0, matrix products: 35.4 us -> none  [the longest x1 9.02 us: shards(): jnp.einsum('hik,hij->khj', left_full, grad_heads, preferred_element_type=...]
    all_gather x1 -> x0, local copies, waits for them, and re-layouts: 18.4 us -> none  [shards(): left_full = lax.all_gather(left_heads, 'col', axis=2, tiled=True)]
    reduce_sum x4 -> x0, other arithmetic: 6.65 us -> none  [the longest x1 2.69 us: norm_back(): jnp.mean(grad, -1, keepdims=True)]
  transfers between devices with their start and end apart: 4 -> 0, of which waited for: 4 -> 0; matrix products, arithmetic and copies ran while one was open for 12% -> 0% of each run, Pallas kernels for 0% -> 0%
where the time goes in v1:
time: 96.5 us; the launch traced here: 96.3 us
  Pallas kernels  89.4 us (93%)
  local copies, waits for them, and re-layouts  6.24 us (6%)
    pallas_call x1, Pallas kernels, shards(): pl.pallas_call(kernel, out_shape=(jax.ShapeDtypeStruct(cells, F32), jax.S...  89.4 us
    unnamed x7, local copies, waits for them, and re-layouts  6.24 us

profile of v1, /device:TPU:1, one launch (start us, length us, event | category | flops | bytes accessed | tf_op | source)
XLA Modules:
  0.0 96.3 jit_solution(12263601725696080251)
XLA Ops:
  0.6 89.4 %shard_map.103 = (f32[64,64,128]{2,1,0:T(8,128)}, f32[64,64,128]{2,1,0:T(8,128)}, bf16[64,64,128]{2,1,0:T(8,128)(2,1)}) custom-call(f32[64,64,128]{2,1,0:T(8,128)} %pair_hbm.1, bf16[64,64,128]{2,1,0:T(8,128)(2,1)} %bitcast.6, bf16[64,128]{1,0:T(8,128)(2,1)} %bitcast.7, bf16[64,128]{1,0:T(8,128)(2,1)} %bitcast.8, bf16[128,128]{1,0:T(8,128)(2,1)} %wg_ref.1, ...), custom_call_target="tpu_custom_call" | custom-call | tf_op jit(solution)/shard_map/pallas_call | solution.py:346
  90.0 0.0 copy-start
  90.0 3.3 %copy.14 = f32[64,64,128]{2,1,0:T(8,128)} copy(f32[64,64,128]{2,1,0:T(8,128)} %get-tuple-element.12) | data formatting | bytes 4194304
  93.3 0.0 copy-done
  93.3 0.0 copy-start.1
  93.3 1.3 %copy.15 = f32[64,64,128]{2,1,0:T(8,128)} copy(f32[64,64,128]{2,1,0:T(8,128)S(1)} %copy-done) | data formatting | bytes 4194304
  94.7 0.6 copy-done.1
  95.3 1.0 %copy.16 = bf16[64,128,64]{1,2,0:T(8,128)(2,1)} copy(bf16[64,128,64]{1,2,0:T(8,128)(2,1)S(1)} %bitcast.5) | data formatting | bytes 2097152
Async XLA Ops:
  90.0 3.3 %copy-start = (f32[64,64,128]{2,1,0:T(8,128)S(1)}, f32[64,64,128]{2,1,0:T(8,128)}, u32[]{:S(2)}) copy-start(f32[64,64,128]{2,1,0:T(8,128)} %get-tuple-element.13) | copy-start | bytes 6291460
  93.3 2.0 %copy-start.1 = (bf16[64,64,128]{2,1,0:T(8,128)(2,1)S(1)}, bf16[64,64,128]{2,1,0:T(8,128)(2,1)}, u32[]{:S(2)}) copy-start(bf16[64,64,128]{2,1,0:T(8,128)(2,1)} %get-tuple-element.8) | copy-start | bytes 3145732

commit v2 on v1

v2 whole, which is shorter than its diff:
```python
import functools

import jax
import jax.numpy as jnp
from jax import lax
from jax.experimental import pallas as pl
from jax.experimental.pallas import tpu as pltpu
from jax.sharding import PartitionSpec as P

EPS = 1e-05
F32 = jnp.float32
BF16 = jnp.bfloat16
MESH = pl.DeviceIdType.MESH

CH = 128
HID = 64
SIDE = 64
ROW = 8
COLC = 8
HALF = SIDE // 2
KB = 128
LANES = 128
PEERS = ROW * COLC
NCH = 2
SB = HALF // NCH
TR = ROW * 2 * SB
UNROLL = 2


def dot(a, b, da, db):
    return lax.dot_general(a, b, (((da,), (db,)), ((), ())), preferred_element_type=F32)


def swap(a, b):
    left = lax.broadcasted_iota(jnp.int32, a.shape, a.ndim - 1) < LANES // 2
    ra = pltpu.roll(a, LANES // 2, a.ndim - 1)
    rb = pltpu.roll(b, LANES // 2, b.ndim - 1)
    return jnp.where(left, a, rb), jnp.where(left, ra, b)


def kernel(
    pair_hbm, right_hbm, wlg_ref, wl_ref, wg_ref, gain_ref, wo_ref, cot_hbm,
    upd, gp, gr,
    xn, cot, inv, gate, sig, val, dgate,
    stage, send_l, lb, lfull, rt, tm, tr, dts, dtr, dtfull, grs, dlk, dlx, dly, dls, dlr, wcat, gcol,
    io_sem, send_sem, recv_sem, tri_sem, stage_sem,
):
    row, col = lax.axis_index("row"), lax.axis_index("col")
    core = lax.rem(col, 2)
    colc = col // 2
    me = row * COLC + colc
    sibling = (row, colc * 2 + (1 - core))

    def peer(off):
        prow = lax.rem(row + off // COLC, ROW)
        pcol = lax.rem(colc + lax.rem(off, COLC), COLC)
        return prow * COLC + pcol, (prow, pcol * 2 + core)

    load_pair = pltpu.make_async_copy(pair_hbm, xn, io_sem.at[0])
    load_pair.start()
    load_cot = pltpu.make_async_copy(cot_hbm, cot, io_sem.at[1])
    load_cot.start()

    barrier = pltpu.get_barrier_semaphore()

    def greet(off, _):
        pl.semaphore_signal(barrier, inc=1, device_id=peer(off)[1], device_id_type=MESH)
        pl.semaphore_signal(barrier, inc=1, device_id=peer(off * COLC)[1], device_id_type=MESH)
        return 0

    def greet_again(off, _):
        pl.semaphore_signal(stage_sem, inc=1, device_id=peer(off * COLC)[1], device_id_type=MESH)
        return 0

    lax.fori_loop(1, ROW, greet, 0)
    pl.semaphore_signal(barrier, inc=1, device_id=sibling, device_id_type=MESH)

    def exchange(src_of, dst, send, recv, lo=1, hi=PEERS):
        if lo == 1:
            pltpu.make_async_copy(src_of(me), dst, recv).start()

        def one(off, _):
            q, device = peer(off)
            pltpu.make_async_remote_copy(
                src_ref=src_of(q),
                dst_ref=dst,
                send_sem=send,
                recv_sem=recv,
                device_id=device,
                device_id_type=MESH,
            ).start()
            return 0

        lax.fori_loop(lo, hi, one, 0)

    def arrived(buf, sem):
        pltpu.make_async_copy(buf, buf, sem).wait()

    def sent(buf, sem):
        part = buf.at[pl.ds(0, PEERS - 1)]
        pltpu.make_async_copy(part, part, sem).wait()

    wcat[:HID] = wl_ref[...]
    wcat[HID:] = wlg_ref[...]
    eye = lax.broadcasted_iota(jnp.int32, (HID, HID), 0) == lax.broadcasted_iota(jnp.int32, (HID, HID), 1)
    column = jnp.sum(jnp.where(eye, gain_ref[...], 0.0), axis=1, keepdims=True)
    gcol[...] = jnp.broadcast_to(column, (HID, LANES))

    load_pair.wait()

    def stage_rows(s):
        return pl.ds((s // SB) * (HID * SB) + lax.rem(s, SB), HID, stride=SB)

    def left_step(s, _):
        x = jnp.concatenate([xn[s], xn[s + HALF]], axis=0)
        centred = x - jnp.mean(x, -1, keepdims=True)
        inv_std = lax.rsqrt(jnp.mean(centred * centred, -1, keepdims=True) + EPS)
        normed = centred * inv_std
        xn[s] = normed[:SIDE]
        xn[s + HALF] = normed[SIDE:]
        inv[s] = jnp.broadcast_to(inv_std, (LANES, CH))
        both = dot(wcat[...], normed.astype(BF16), 1, 1)
        value = both[:HID]
        left_sig = jax.nn.sigmoid(both[HID:])
        val[s] = value
        sig[s] = left_sig
        stage[stage_rows(s), :] = left_sig * value
        return 0

    lax.fori_loop(0, SB, left_step, 0, unroll=UNROLL)
    pl.semaphore_wait(barrier, 2 * ROW - 1)
    lax.fori_loop(1, ROW, greet_again, 0)
    lax.fori_loop(SB, HALF, left_step, 0, unroll=UNROLL)

    def stage_block(t, h):
        return pl.ds(pl.multiple_of((t * HID + h) * SB, SB), SB)

    def pack_left(h, _):
        send_l[h] = jnp.concatenate([stage[stage_block(t, h), :] for t in range(NCH)], axis=0).astype(BF16)
        return 0

    lax.fori_loop(0, HID, pack_left, 0, unroll=4)
    pl.semaphore_wait(stage_sem, ROW - 1)
    exchange(lambda q: send_l.at[q], lb.at[core, me], send_sem.at[1], recv_sem.at[1])
    exchange(lambda q: right_hbm.at[q], rt.at[me], send_sem.at[0], recv_sem.at[0])

    def gate_step(s, _):
        low = jnp.concatenate([xn[s], xn[s + HALF]], axis=0).astype(BF16)
        gate[s] = jax.nn.sigmoid(dot(low, wg_ref[...], 1, 0))
        return 0

    lax.fori_loop(0, HALF, gate_step, 0, unroll=UNROLL)

    arrived(lb.at[core], recv_sem.at[1])
    swap_left = pltpu.make_async_remote_copy(
        src_ref=lb.at[core],
        dst_ref=lb.at[core],
        send_sem=send_sem.at[2],
        recv_sem=recv_sem.at[2],
        device_id=sibling,
        device_id_type=MESH,
    )
    swap_left.start()
    arrived(lb.at[1 - core], recv_sem.at[2])

    def unpack_left(q, _):
        r, c = q // COLC, lax.rem(q, COLC)
        top, bottom = swap(lb[0, q].astype(F32), lb[1, q].astype(F32))
        for t in range(NCH):
            block = jnp.concatenate([top[t * SB : (t + 1) * SB], bottom[t * SB : (t + 1) * SB]], axis=0)
            at = pl.multiple_of(t * TR + r * 2 * SB, 2 * SB)
            lfull[c, pl.ds(at, 2 * SB), :] = block.astype(BF16)
        return 0

    lax.fori_loop(0, PEERS, unpack_left, 0, unroll=2)

    def k_left(lo, rows=slice(None)):
        return jnp.concatenate([lfull[lo, rows], lfull[lo + 1, rows]], axis=1)

    def k_right(lo):
        a = jnp.concatenate([rt[lo * COLC + c] for c in range(COLC)], axis=0)
        b = jnp.concatenate([rt[(lo + 1) * COLC + c] for c in range(COLC)], axis=0)
        return jnp.concatenate([a, b], axis=1)

    arrived(rt, recv_sem.at[0])

    for t in range(NCH):
        rows = slice(t * TR, (t + 1) * TR)
        total = dot(k_left(0, rows), k_right(0), 1, 1)
        for lo in range(2, ROW, 2):
            total += dot(k_left(lo, rows), k_right(lo), 1, 1)
        for r in range(ROW):
            for p in range(COLC // 2):
                lanes = slice(p * LANES, (p + 1) * LANES)
                a, b = swap(
                    total[r * 2 * SB : r * 2 * SB + SB, lanes],
                    total[r * 2 * SB + SB : (r + 1) * 2 * SB, lanes],
                )
                tm[t, r * COLC + 2 * p] = a.astype(BF16)
                tm[t, r * COLC + 2 * p + 1] = b.astype(BF16)
        exchange(lambda q: tm.at[t, q], tr.at[t, me], tri_sem.at[0, t], tri_sem.at[1, t])

    def widen(buf, t):
        def one(h, _):
            stage[stage_block(t, h), :] = buf[t, h].astype(F32)
            return 0

        lax.fori_loop(0, HID, one, 0, unroll=8)

    def middle_step(s, _):
        tri = stage[stage_rows(s), :]
        centred = tri - jnp.mean(tri, 0, keepdims=True)
        inv_out = lax.rsqrt(jnp.mean(centred * centred, 0, keepdims=True) + EPS)
        hat = centred * inv_out
        gain = gcol[...]
        linear = dot((hat * gain).astype(BF16), wo_ref[...], 0, 0)
        g = gate[s]
        update = g * linear
        upd[s] = update[:SIDE]
        upd[s + HALF] = update[SIDE:]
        ct = jnp.concatenate([cot[s], cot[s + HALF]], axis=0)
        d_linear = ct * g
        dgate[s] = (ct * linear * g * (1.0 - g)).astype(BF16)
        d_scaled = dot(wo_ref[...], d_linear.astype(BF16), 1, 1) * gain
        d_tri = inv_out * (
            d_scaled
            - jnp.mean(d_scaled, 0, keepdims=True)
            - hat * jnp.mean(d_scaled * hat, 0, keepdims=True)
        )
        stage[stage_rows(s), :] = d_tri
        return 0

    load_cot.wait()
    for t in range(NCH):
        arrived(tr.at[t], tri_sem.at[1, t])
        widen(tr, t)
        lax.fori_loop(t * SB, (t + 1) * SB, middle_step, 0, unroll=UNROLL)

        def pack_tri(h, _):
            dts[t, h] = stage[stage_block(t, h), :].astype(BF16)
            return 0

        lax.fori_loop(0, HID, pack_tri, 0, unroll=8)
        exchange(lambda q: dts.at[t, q], dtr.at[t, me], tri_sem.at[2, t], tri_sem.at[3, t])

    def swap_grad(t):
        return pltpu.make_async_remote_copy(
            src_ref=dlx.at[t],
            dst_ref=dly.at[t],
            send_sem=tri_sem.at[4, t],
            recv_sem=tri_sem.at[5, t],
            device_id=sibling,
            device_id_type=MESH,
        )

    def left_grad(t):
        arrived(dtr.at[t], tri_sem.at[3, t])

        def unpack_tri(n, _):
            r, p = n // (COLC // 2), lax.rem(n, COLC // 2)
            at = r * COLC + 2 * p
            top, bottom = swap(dtr[t, at].astype(F32), dtr[t, at + 1].astype(F32))
            block = jnp.concatenate([top, bottom], axis=0).astype(BF16)
            dtfull[p, pl.ds(pl.multiple_of(t * TR + r * 2 * SB, 2 * SB), 2 * SB), :] = block
            return 0

        lax.fori_loop(0, PEERS // 2, unpack_tri, 0, unroll=4)
        d_tri = jnp.concatenate([dtfull[p, t * TR : (t + 1) * TR] for p in range(COLC // 2)], axis=1)
        for lo in range(0, ROW, 2):
            part = dot(d_tri, k_right(lo), 1, 0)
            for c in range(2):
                for r in range(ROW):
                    lanes = slice(c * LANES, (c + 1) * LANES)
                    for_0, for_1 = swap(
                        part[r * 2 * SB : r * 2 * SB + SB, lanes],
                        part[r * 2 * SB + SB : (r + 1) * 2 * SB, lanes],
                    )
                    at = r * COLC + lo + c
                    first = core == 0
                    dlk[t, at] = jnp.where(first, for_0, for_1)
                    dlx[t, at] = jnp.where(first, for_1, for_0).astype(BF16)
        swap_grad(t).start()

    def send_left_grad(t):
        swap_grad(t).wait_recv()

        def add_halves(q, _):
            dls[t, q] = (dlk[t, q] + dly[t, q].astype(F32)).astype(BF16)
            return 0

        lax.fori_loop(0, PEERS, add_halves, 0, unroll=8)
        exchange(lambda q: dls.at[t, q], dlr.at[t, me], tri_sem.at[6, t], tri_sem.at[7, t])

    for t in range(NCH - 1):
        left_grad(t)
        send_left_grad(t)
    left_grad(NCH - 1)

    d_tri_all = jnp.concatenate([dtfull[p] for p in range(COLC // 2)], axis=1)
    for lo in range(0, COLC, 2):
        part = dot(d_tri_all, k_left(lo), 0, 0).astype(BF16)
        for c in range(2):
            for cc in range(COLC):
                grs[(lo + c) * COLC + cc] = part[cc * SIDE : (cc + 1) * SIDE, c * LANES : (c + 1) * LANES]

    def send_right_grad(lo, hi):
        exchange(lambda q: grs.at[q], gr.at[me], send_sem.at[3], recv_sem.at[3], lo, hi)

    send_right_grad(1, PEERS // 2)
    send_left_grad(NCH - 1)
    send_right_grad(PEERS // 2, PEERS)

    def final_step(s, _):
        d_left = stage[stage_rows(s), :]
        left_sig, value = sig[s], val[s]
        d_value = d_left * left_sig
        d_logit = d_left * value * left_sig * (1.0 - left_sig)
        stacked = jnp.concatenate([d_value, d_logit], axis=0).astype(BF16)
        grad = dot(stacked, wcat[...], 0, 0) + dot(dgate[s], wg_ref[...], 1, 1)
        normed = jnp.concatenate([xn[s], xn[s + HALF]], axis=0)
        out = inv[s] * (
            grad
            - jnp.mean(grad, -1, keepdims=True)
            - normed * jnp.mean(grad * normed, -1, keepdims=True)
        )
        gp[s] = out[:SIDE]
        gp[s + HALF] = out[SIDE:]
        return 0

    for t in range(NCH):
        arrived(dlr.at[t], tri_sem.at[7, t])
        widen(dlr, t)
        lax.fori_loop(t * SB, (t + 1) * SB, final_step, 0, unroll=UNROLL)

    sent(right_hbm, send_sem.at[0])
    sent(send_l, send_sem.at[1])
    swap_left.wait_send()
    for t in range(NCH):
        sent(tm.at[t], tri_sem.at[0, t])
        sent(dts.at[t], tri_sem.at[2, t])
        swap_grad(t).wait_send()
        sent(dls.at[t], tri_sem.at[6, t])
    sent(grs, send_sem.at[3])
    arrived(gr, recv_sem.at[3])


def shards(pair, right_proj, w_left_gate, w_left, w_gate, out_gain, w_out, cotangent):
    any_spec = pl.BlockSpec(memory_space=pl.ANY)
    vmem = pl.BlockSpec(memory_space=pltpu.VMEM)
    cells = (SIDE, SIDE, CH)
    block8 = (PEERS, HALF, LANES)
    chunks = (NCH, PEERS, SB, LANES)
    block16 = (PEERS, SIDE, KB)
    per_step = (HALF, LANES, CH)
    heads = (HALF, HID, LANES)
    scratch = [
        (cells, F32), (cells, F32), (per_step, F32), (per_step, F32), (heads, F32), (heads, F32),
        (per_step, BF16),
        ((HID * HALF, LANES), F32),
        (block8, BF16),
        ((2,) + block8, BF16),
        ((COLC, ROW * SIDE, LANES), BF16),
        (block16, BF16),
        (chunks, BF16), (chunks, BF16), (chunks, BF16), (chunks, BF16),
        ((COLC // 2, ROW * SIDE, LANES), BF16),
        (block16, BF16),
        (chunks, F32),
        (chunks, BF16), (chunks, BF16), (chunks, BF16), (chunks, BF16),
        ((2 * HID, CH), BF16),
        ((HID, LANES), F32),
    ]
    update, grad_pair, grad_right = pl.pallas_call(
        kernel,
        out_shape=(pltpu.VMEM(cells, F32), pltpu.VMEM(cells, F32), pltpu.VMEM((HID, SIDE, KB), BF16)),
        in_specs=[any_spec, any_spec, vmem, vmem, vmem, vmem, vmem, any_spec],
        out_specs=(vmem, vmem, vmem),
        scratch_shapes=[pltpu.VMEM(shape, dtype) for shape, dtype in scratch]
        + [
            pltpu.SemaphoreType.DMA((2,)),
            pltpu.SemaphoreType.DMA((4,)),
            pltpu.SemaphoreType.DMA((4,)),
            pltpu.SemaphoreType.DMA((8, NCH)),
            pltpu.SemaphoreType.REGULAR,
        ],
        compiler_params=pltpu.CompilerParams(
            collective_id=0, has_side_effects=True, vmem_limit_bytes=58 * 1024 * 1024
        ),
    )(
        pair,
        jnp.transpose(right_proj, (0, 2, 1)),
        w_left_gate.T,
        w_left.T,
        w_gate,
        out_gain.reshape(1, HID),
        w_out,
        cotangent,
    )
    return update, grad_pair, jnp.transpose(grad_right, (0, 2, 1))


def solution(mesh):
    in_specs = (
        P("row", "col", None),
        P(None, "row", "col"),
        P(),
        P(),
        P(),
        P(),
        P(),
        P("row", "col", None),
    )
    out_specs = (P("row", "col", None), P("row", "col", None), P(None, "row", "col"))
    return jax.shard_map(shards, mesh=mesh, in_specs=in_specs, out_specs=out_specs, check_vma=False)
```

time: 96.5 us -> 85.1 us (0.88); the launches traced: 96.3 us -> 83.5 us
  Pallas kernels: 89.4 us -> 79.2 us
  local copies, waits for them, and re-layouts: 6.24 us -> 3.61 us
    pallas_call x1, Pallas kernels: 89.4 us -> 79.2 us  [shards(): pl.pallas_call(kernel, out_shape=(pltpu.VMEM(cells, F32), pltpu.VMEM(cell...]
    unnamed x7 -> x3, local copies, waits for them, and re-layouts: 6.24 us -> 3.61 us
where the time goes in v2:
time: 85.1 us; the launch traced here: 83.5 us
  Pallas kernels  79.2 us (93%)
  local copies, waits for them, and re-layouts  3.61 us (4%)
    pallas_call x1, Pallas kernels, shards(): pl.pallas_call(kernel, out_shape=(pltpu.VMEM(cells, F32), pltpu.VMEM(cell...  79.2 us
    unnamed x3, local copies, waits for them, and re-layouts  3.61 us

profile of v2, /device:TPU:1, one launch (start us, length us, event | category | flops | bytes accessed | tf_op | source)
XLA Modules:
  0.0 83.5 jit_solution(2144973388428535552)
XLA Ops:
  0.6 79.2 %shard_map.103 = (f32[64,64,128]{2,1,0:T(8,128)S(1)}, f32[64,64,128]{2,1,0:T(8,128)S(1)}, bf16[64,64,128]{2,1,0:T(8,128)(2,1)S(1)}) custom-call(f32[64,64,128]{2,1,0:T(8,128)} %pair_hbm.1, bf16[64,64,128]{2,1,0:T(8,128)(2,1)} %bitcast.6, bf16[64,128]{1,0:T(8,128)(2,1)} %bitcast.7, bf16[64,128]{1,0:T(8,128)(2,1)} %bitcast.8, bf16[128,128]{1,0:T(8,128)(2,1)} %wg_ref.1, ...), custom_call_target="tpu_custom_call" | custom-call | tf_op jit(solution)/shard_map/pallas_call | solution.py:372
  79.9 1.3 %copy.14 = f32[64,64,128]{2,1,0:T(8,128)} copy(f32[64,64,128]{2,1,0:T(8,128)S(1)} %get-tuple-element.9) | data formatting | bytes 4194304
  81.2 1.0 %copy.16 = bf16[64,128,64]{1,2,0:T(8,128)(2,1)} copy(bf16[64,128,64]{1,2,0:T(8,128)(2,1)S(1)} %bitcast.5) | data formatting | bytes 2097152
  82.1 1.3 %copy.15 = f32[64,64,128]{2,1,0:T(8,128)} copy(f32[64,64,128]{2,1,0:T(8,128)S(1)} %get-tuple-element.10) | data formatting | bytes 4194304

commit v3 on v2

--- a/solution.py
+++ b/solution.py
@@ -1,4 +1,4 @@
-import functools
+import random
 
 import jax
 import jax.numpy as jnp
@@ -24,7 +24,15 @@
 NCH = 2
 SB = HALF // NCH
 TR = ROW * 2 * SB
-UNROLL = 2
+UNROLL = 8
+STEPS = (0, 1, 2, -1)
+OTHERS = [(x, y, z) for x in STEPS for y in STEPS for z in STEPS if (x, y, z) != (0, 0, 0)]
+random.Random(1).shuffle(OTHERS)
+OTHERS.sort(key=lambda v: -sum(map(abs, v)))
+PLANE = [v for v in OTHERS if v[2] == 0]
+LINE = [v for v in OTHERS if v[0] == 0 and v[1] == 0]
+NEAR = [v for v in OTHERS if v in PLANE or v in LINE]
+REST = [v for v in OTHERS if v not in NEAR]
 
 
 def dot(a, b, da, db):
@@ -43,7 +51,7 @@
     upd, gp, gr,
     xn, cot, inv, gate, sig, val, dgate,
     stage, send_l, lb, lfull, rt, tm, tr, dts, dtr, dtfull, grs, dlk, dlx, dly, dls, dlr, wcat, gcol,
-    io_sem, send_sem, recv_sem, tri_sem, stage_sem,
+    io_sem, send_sem, recv_sem, tri_sem, line_sem,
 ):
     row, col = lax.axis_index("row"), lax.axis_index("col")
     core = lax.rem(col, 2)
@@ -51,9 +59,15 @@
     me = row * COLC + colc
     sibling = (row, colc * 2 + (1 - core))
 
-    def peer(off):
-        prow = lax.rem(row + off // COLC, ROW)
-        pcol = lax.rem(colc + lax.rem(off, COLC), COLC)
+    across = {d: lax.rem(colc // 2 + d + 4, 4) for d in STEPS}
+    up = {d: lax.rem(lax.rem(colc, 2) * 2 + row // 4 + d + 4, 4) for d in STEPS}
+    deep = {d: lax.rem(lax.rem(row, 4) + d + 4, 4) for d in STEPS}
+    cols = {(x, y): across[x] * 2 + up[y] // 2 for x in STEPS for y in STEPS}
+    rows_of = {(y, z): lax.rem(up[y], 2) * 4 + deep[z] for y in STEPS for z in STEPS}
+
+    def peer(v):
+        x, y, z = v
+        prow, pcol = rows_of[y, z], cols[x, y]
         return prow * COLC + pcol, (prow, pcol * 2 + core)
 
     load_pair = pltpu.make_async_copy(pair_hbm, xn, io_sem.at[0])
@@ -62,25 +76,16 @@
     load_cot.start()
 
     barrier = pltpu.get_barrier_semaphore()
-
-    def greet(off, _):
-        pl.semaphore_signal(barrier, inc=1, device_id=peer(off)[1], device_id_type=MESH)
-        pl.semaphore_signal(barrier, inc=1, device_id=peer(off * COLC)[1], device_id_type=MESH)
-        return 0
-
-    def greet_again(off, _):
-        pl.semaphore_signal(stage_sem, inc=1, device_id=peer(off * COLC)[1], device_id_type=MESH)
-        return 0
-
-    lax.fori_loop(1, ROW, greet, 0)
+    for v in NEAR:
+        pl.semaphore_signal(barrier, inc=1, device_id=peer(v)[1], device_id_type=MESH)
     pl.semaphore_signal(barrier, inc=1, device_id=sibling, device_id_type=MESH)
 
-    def exchange(src_of, dst, send, recv, lo=1, hi=PEERS):
-        if lo == 1:
-            pltpu.make_async_copy(src_of(me), dst, recv).start()
-
-        def one(off, _):
-            q, device = peer(off)
+    def keep(src_of, dst, recv):
+        pltpu.make_async_copy(src_of(me), dst, recv).start()
+
+    def exchange(src_of, dst, send, recv, others=OTHERS):
+        for v in others:
+            q, device = peer(v)
             pltpu.make_async_remote_copy(
                 src_ref=src_of(q),
                 dst_ref=dst,
@@ -89,9 +94,6 @@
                 device_id=device,
                 device_id_type=MESH,
             ).start()
-            return 0
-
-        lax.fori_loop(lo, hi, one, 0)
 
     def arrived(buf, sem):
         pltpu.make_async_copy(buf, buf, sem).wait()
@@ -128,8 +130,15 @@
         return 0
 
     lax.fori_loop(0, SB, left_step, 0, unroll=UNROLL)
-    pl.semaphore_wait(barrier, 2 * ROW - 1)
-    lax.fori_loop(1, ROW, greet_again, 0)
+    pl.semaphore_wait(barrier, len(NEAR) + 1)
+    for v in LINE:
+        pl.semaphore_signal(line_sem, inc=1, device_id=peer(v)[1], device_id_type=MESH)
+
+    def send_right(others):
+        exchange(lambda q: right_hbm.at[q], rt.at[me], send_sem.at[0], recv_sem.at[0], others)
+
+    keep(lambda q: right_hbm.at[q], rt.at[me], recv_sem.at[0])
+    send_right(NEAR)
     lax.fori_loop(SB, HALF, left_step, 0, unroll=UNROLL)
 
     def stage_block(t, h):
@@ -140,9 +149,10 @@
         return 0
 
     lax.fori_loop(0, HID, pack_left, 0, unroll=4)
-    pl.semaphore_wait(stage_sem, ROW - 1)
+    pl.semaphore_wait(line_sem, len(LINE))
+    keep(lambda q: send_l.at[q], lb.at[core, me], recv_sem.at[1])
     exchange(lambda q: send_l.at[q], lb.at[core, me], send_sem.at[1], recv_sem.at[1])
-    exchange(lambda q: right_hbm.at[q], rt.at[me], send_sem.at[0], recv_sem.at[0])
+    send_right(REST)
 
     def gate_step(s, _):
         low = jnp.concatenate([xn[s], xn[s + HALF]], axis=0).astype(BF16)
@@ -172,7 +182,7 @@
             lfull[c, pl.ds(at, 2 * SB), :] = block.astype(BF16)
         return 0
 
-    lax.fori_loop(0, PEERS, unpack_left, 0, unroll=2)
+    lax.fori_loop(0, PEERS, unpack_left, 0, unroll=4)
 
     def k_left(lo, rows=slice(None)):
         return jnp.concatenate([lfull[lo, rows], lfull[lo + 1, rows]], axis=1)
@@ -198,6 +208,9 @@
                 )
                 tm[t, r * COLC + 2 * p] = a.astype(BF16)
                 tm[t, r * COLC + 2 * p + 1] = b.astype(BF16)
+        if t:
+            sent(tm.at[t - 1], tri_sem.at[0, t - 1])
+        keep(lambda q: tm.at[t, q], tr.at[t, me], tri_sem.at[1, t])
         exchange(lambda q: tm.at[t, q], tr.at[t, me], tri_sem.at[0, t], tri_sem.at[1, t])
 
     def widen(buf, t):
@@ -241,6 +254,7 @@
             return 0
 
         lax.fori_loop(0, HID, pack_tri, 0, unroll=8)
+        keep(lambda q: dts.at[t, q], dtr.at[t, me], tri_sem.at[3, t])
         exchange(lambda q: dts.at[t, q], dtr.at[t, me], tri_sem.at[2, t], tri_sem.at[3, t])
 
     def swap_grad(t):
@@ -253,7 +267,7 @@
             device_id_type=MESH,
         )
 
-    def left_grad(t):
+    def tri_grad(t):
         arrived(dtr.at[t], tri_sem.at[3, t])
 
         def unpack_tri(n, _):
@@ -264,7 +278,9 @@
             dtfull[p, pl.ds(pl.multiple_of(t * TR + r * 2 * SB, 2 * SB), 2 * SB), :] = block
             return 0
 
-        lax.fori_loop(0, PEERS // 2, unpack_tri, 0, unroll=4)
+        lax.fori_loop(0, PEERS // 2, unpack_tri, 0, unroll=8)
+
+    def left_grad(t):
         d_tri = jnp.concatenate([dtfull[p, t * TR : (t + 1) * TR] for p in range(COLC // 2)], axis=1)
         for lo in range(0, ROW, 2):
             part = dot(d_tri, k_right(lo), 1, 0)
@@ -289,12 +305,14 @@
             return 0
 
         lax.fori_loop(0, PEERS, add_halves, 0, unroll=8)
+        keep(lambda q: dls.at[t, q], dlr.at[t, me], tri_sem.at[7, t])
         exchange(lambda q: dls.at[t, q], dlr.at[t, me], tri_sem.at[6, t], tri_sem.at[7, t])
 
     for t in range(NCH - 1):
+        tri_grad(t)
         left_grad(t)
         send_left_grad(t)
-    left_grad(NCH - 1)
+    tri_grad(NCH - 1)
 
     d_tri_all = jnp.concatenate([dtfull[p] for p in range(COLC // 2)], axis=1)
     for lo in range(0, COLC, 2):
@@ -303,12 +321,15 @@
             for cc in range(COLC):
                 grs[(lo + c) * COLC + cc] = part[cc * SIDE : (cc + 1) * SIDE, c * LANES : (c + 1) * LANES]
 
-    def send_right_grad(lo, hi):
-        exchange(lambda q: grs.at[q], gr.at[me], send_sem.at[3], recv_sem.at[3], lo, hi)
-
-    send_right_grad(1, PEERS // 2)
+    def send_right_grad(others):
+        exchange(lambda q: grs.at[q], gr.at[me], send_sem.at[3], recv_sem.at[3], others)
+
+    keep(lambda q: grs.at[q], gr.at[me], recv_sem.at[3])
+    send_right_grad(OTHERS[0::2])
+    left_grad(NCH - 1)
     send_left_grad(NCH - 1)
-    send_right_grad(PEERS // 2, PEERS)
+    sent(dls.at[NCH - 1], tri_sem.at[6, NCH - 1])
+    send_right_grad(OTHERS[1::2])
 
     def final_step(s, _):
         d_left = stage[stage_rows(s), :]
@@ -336,9 +357,10 @@
     sent(send_l, send_sem.at[1])
     swap_left.wait_send()
     for t in range(NCH):
-        sent(tm.at[t], tri_sem.at[0, t])
         sent(dts.at[t], tri_sem.at[2, t])
         swap_grad(t).wait_send()
+    sent(tm.at[NCH - 1], tri_sem.at[0, NCH - 1])
+    for t in range(NCH - 1):
         sent(dls.at[t], tri_sem.at[6, t])
     sent(grs, send_sem.at[3])
     arrived(gr, recv_sem.at[3])

time: 85.1 us -> 79.5 us (0.934); the launches traced: 83.5 us -> 79.3 us
  Pallas kernels: 79.2 us -> 75.1 us
    pallas_call x1, Pallas kernels: 79.2 us -> 75.1 us  [shards(): pl.pallas_call(kernel, out_shape=(pltpu.VMEM(cells, F32), pltpu.VMEM(cell...]
where the time goes in v3:
time: 79.5 us; the launch traced here: 79.3 us
  Pallas kernels  75.1 us (94%)
  local copies, waits for them, and re-layouts  3.61 us (5%)
    pallas_call x1, Pallas kernels, shards(): pl.pallas_call(kernel, out_shape=(pltpu.VMEM(cells, F32), pltpu.VMEM(cell...  75.1 us
    unnamed x3, local copies, waits for them, and re-layouts  3.61 us

profile of v3, /device:TPU:1, one launch (start us, length us, event | category | flops | bytes accessed | tf_op | source)
XLA Modules:
  0.0 79.3 jit_solution(7625011103847663141)
XLA Ops:
  0.6 75.1 %shard_map.103 = (f32[64,64,128]{2,1,0:T(8,128)S(1)}, f32[64,64,128]{2,1,0:T(8,128)S(1)}, bf16[64,64,128]{2,1,0:T(8,128)(2,1)S(1)}) custom-call(f32[64,64,128]{2,1,0:T(8,128)} %pair_hbm.1, bf16[64,64,128]{2,1,0:T(8,128)(2,1)} %bitcast.6, bf16[64,128]{1,0:T(8,128)(2,1)} %bitcast.7, bf16[64,128]{1,0:T(8,128)(2,1)} %bitcast.8, bf16[128,128]{1,0:T(8,128)(2,1)} %wg_ref.1, ...), custom_call_target="tpu_custom_call" | custom-call | tf_op jit(solution)/shard_map/pallas_call | solution.py:394
  75.7 1.3 %copy.14 = f32[64,64,128]{2,1,0:T(8,128)} copy(f32[64,64,128]{2,1,0:T(8,128)S(1)} %get-tuple-element.9) | data formatting | bytes 4194304
  77.1 1.0 %copy.16 = bf16[64,128,64]{1,2,0:T(8,128)(2,1)} copy(bf16[64,128,64]{1,2,0:T(8,128)(2,1)S(1)} %bitcast.5) | data formatting | bytes 2097152
  78.0 1.3 %copy.15 = f32[64,64,128]{2,1,0:T(8,128)} copy(f32[64,64,128]{2,1,0:T(8,128)S(1)} %get-tuple-element.10) | data formatting | bytes 4194304

commit v4 on v3

--- a/solution.py
+++ b/solution.py
@@ -24,7 +24,7 @@
 NCH = 2
 SB = HALF // NCH
 TR = ROW * 2 * SB
-UNROLL = 8
+UNROLL = 16
 STEPS = (0, 1, 2, -1)
 OTHERS = [(x, y, z) for x in STEPS for y in STEPS for z in STEPS if (x, y, z) != (0, 0, 0)]
 random.Random(1).shuffle(OTHERS)
@@ -32,7 +32,7 @@
 PLANE = [v for v in OTHERS if v[2] == 0]
 LINE = [v for v in OTHERS if v[0] == 0 and v[1] == 0]
 NEAR = [v for v in OTHERS if v in PLANE or v in LINE]
-REST = [v for v in OTHERS if v not in NEAR]
+REST = [v for v in OTHERS if v not in LINE]
 
 
 def dot(a, b, da, db):
@@ -49,8 +49,8 @@
 def kernel(
     pair_hbm, right_hbm, wlg_ref, wl_ref, wg_ref, gain_ref, wo_ref, cot_hbm,
     upd, gp, gr,
-    xn, cot, inv, gate, sig, val, dgate,
-    stage, send_l, lb, lfull, rt, tm, tr, dts, dtr, dtfull, grs, dlk, dlx, dly, dls, dlr, wcat, gcol,
+    raw, xn, cot, inv, gate, sig, val, dgate,
+    stage, stage_d, send_l, lb, lfull, rt, tm, tr, dts, dtr, dtfull, grs, dlk, dlx, dly, dls, dlr, wcat, gcol,
     io_sem, send_sem, recv_sem, tri_sem, line_sem,
 ):
     row, col = lax.axis_index("row"), lax.axis_index("col")
@@ -70,7 +70,7 @@
         prow, pcol = rows_of[y, z], cols[x, y]
         return prow * COLC + pcol, (prow, pcol * 2 + core)
 
-    load_pair = pltpu.make_async_copy(pair_hbm, xn, io_sem.at[0])
+    load_pair = pltpu.make_async_copy(pair_hbm, raw, io_sem.at[0])
     load_pair.start()
     load_cot = pltpu.make_async_copy(cot_hbm, cot, io_sem.at[1])
     load_cot.start()
@@ -110,11 +110,15 @@
 
     load_pair.wait()
 
-    def stage_rows(s):
-        return pl.ds((s // SB) * (HID * SB) + lax.rem(s, SB), HID, stride=SB)
-
-    def left_step(s, _):
-        x = jnp.concatenate([xn[s], xn[s + HALF]], axis=0)
+    def stage_rows(t, n):
+        return pl.ds(t * (HID * SB) + n, HID, stride=SB)
+
+    def steps(step, t):
+        lax.fori_loop(0, SB, lambda n, _: (step(t, n), 0)[1], 0, unroll=UNROLL)
+
+    def left_step(t, n):
+        s = t * SB + n
+        x = jnp.concatenate([raw[s], raw[s + HALF]], axis=0)
         centred = x - jnp.mean(x, -1, keepdims=True)
         inv_std = lax.rsqrt(jnp.mean(centred * centred, -1, keepdims=True) + EPS)
         normed = centred * inv_std
@@ -126,20 +130,12 @@
         left_sig = jax.nn.sigmoid(both[HID:])
         val[s] = value
         sig[s] = left_sig
-        stage[stage_rows(s), :] = left_sig * value
-        return 0
-
-    lax.fori_loop(0, SB, left_step, 0, unroll=UNROLL)
+        stage[stage_rows(t, n), :] = left_sig * value
+
+    steps(left_step, 0)
     pl.semaphore_wait(barrier, len(NEAR) + 1)
-    for v in LINE:
-        pl.semaphore_signal(line_sem, inc=1, device_id=peer(v)[1], device_id_type=MESH)
-
-    def send_right(others):
-        exchange(lambda q: right_hbm.at[q], rt.at[me], send_sem.at[0], recv_sem.at[0], others)
-
-    keep(lambda q: right_hbm.at[q], rt.at[me], recv_sem.at[0])
-    send_right(NEAR)
-    lax.fori_loop(SB, HALF, left_step, 0, unroll=UNROLL)
+    exchange(lambda q: right_hbm.at[q], rt.at[me], send_sem.at[0], line_sem, LINE)
+    steps(left_step, 1)
 
     def stage_block(t, h):
         return pl.ds(pl.multiple_of((t * HID + h) * SB, SB), SB)
@@ -149,10 +145,11 @@
         return 0
 
     lax.fori_loop(0, HID, pack_left, 0, unroll=4)
-    pl.semaphore_wait(line_sem, len(LINE))
+    arrived(rt.at[pl.ds(0, len(LINE))], line_sem)
     keep(lambda q: send_l.at[q], lb.at[core, me], recv_sem.at[1])
     exchange(lambda q: send_l.at[q], lb.at[core, me], send_sem.at[1], recv_sem.at[1])
-    send_right(REST)
+    keep(lambda q: right_hbm.at[q], rt.at[me], recv_sem.at[0])
+    exchange(lambda q: right_hbm.at[q], rt.at[me], send_sem.at[0], recv_sem.at[0], REST)
 
     def gate_step(s, _):
         low = jnp.concatenate([xn[s], xn[s + HALF]], axis=0).astype(BF16)
@@ -192,7 +189,7 @@
         b = jnp.concatenate([rt[(lo + 1) * COLC + c] for c in range(COLC)], axis=0)
         return jnp.concatenate([a, b], axis=1)
 
-    arrived(rt, recv_sem.at[0])
+    arrived(rt.at[pl.ds(0, PEERS - len(LINE))], recv_sem.at[0])
 
     for t in range(NCH):
         rows = slice(t * TR, (t + 1) * TR)
@@ -220,8 +217,9 @@
 
         lax.fori_loop(0, HID, one, 0, unroll=8)
 
-    def middle_step(s, _):
-        tri = stage[stage_rows(s), :]
+    def middle_step(t, n):
+        s = t * SB + n
+        tri = stage[stage_rows(t, n), :]
         centred = tri - jnp.mean(tri, 0, keepdims=True)
         inv_out = lax.rsqrt(jnp.mean(centred * centred, 0, keepdims=True) + EPS)
         hat = centred * inv_out
@@ -240,17 +238,16 @@
             - jnp.mean(d_scaled, 0, keepdims=True)
             - hat * jnp.mean(d_scaled * hat, 0, keepdims=True)
         )
-        stage[stage_rows(s), :] = d_tri
-        return 0
+        stage_d[stage_rows(t, n), :] = d_tri
 
     load_cot.wait()
     for t in range(NCH):
         arrived(tr.at[t], tri_sem.at[1, t])
         widen(tr, t)
-        lax.fori_loop(t * SB, (t + 1) * SB, middle_step, 0, unroll=UNROLL)
+        steps(middle_step, t)
 
         def pack_tri(h, _):
-            dts[t, h] = stage[stage_block(t, h), :].astype(BF16)
+            dts[t, h] = stage_d[stage_block(t, h), :].astype(BF16)
             return 0
 
         lax.fori_loop(0, HID, pack_tri, 0, unroll=8)
@@ -325,14 +322,14 @@
         exchange(lambda q: grs.at[q], gr.at[me], send_sem.at[3], recv_sem.at[3], others)
 
     keep(lambda q: grs.at[q], gr.at[me], recv_sem.at[3])
-    send_right_grad(OTHERS[0::2])
+    send_right_grad(OTHERS[0::4])
     left_grad(NCH - 1)
     send_left_grad(NCH - 1)
-    sent(dls.at[NCH - 1], tri_sem.at[6, NCH - 1])
-    send_right_grad(OTHERS[1::2])
-
-    def final_step(s, _):
-        d_left = stage[stage_rows(s), :]
+    send_right_grad([v for n, v in enumerate(OTHERS) if n % 4])
+
+    def final_step(t, n):
+        s = t * SB + n
+        d_left = stage[stage_rows(t, n), :]
         left_sig, value = sig[s], val[s]
         d_value = d_left * left_sig
         d_logit = d_left * value * left_sig * (1.0 - left_sig)
@@ -346,12 +343,11 @@
         )
         gp[s] = out[:SIDE]
         gp[s + HALF] = out[SIDE:]
-        return 0
 
     for t in range(NCH):
         arrived(dlr.at[t], tri_sem.at[7, t])
         widen(dlr, t)
-        lax.fori_loop(t * SB, (t + 1) * SB, final_step, 0, unroll=UNROLL)
+        steps(final_step, t)
 
     sent(right_hbm, send_sem.at[0])
     sent(send_l, send_sem.at[1])
@@ -360,10 +356,21 @@
         sent(dts.at[t], tri_sem.at[2, t])
         swap_grad(t).wait_send()
     sent(tm.at[NCH - 1], tri_sem.at[0, NCH - 1])
-    for t in range(NCH - 1):
+    for t in range(NCH):
         sent(dls.at[t], tri_sem.at[6, t])
     sent(grs, send_sem.at[3])
     arrived(gr, recv_sem.at[3])
+
+
+def store(upd, gp, gr, upd_out, gp_out, gr_out, sem):
+    copies = [
+        pltpu.make_async_copy(src, dst, sem.at[n])
+        for n, (src, dst) in enumerate(((upd, upd_out), (gp, gp_out), (gr, gr_out)))
+    ]
+    for copy in copies:
+        copy.start()
+    for copy in copies:
+        copy.wait()
 
 
 def shards(pair, right_proj, w_left_gate, w_left, w_gate, out_gain, w_out, cotangent):
@@ -376,9 +383,9 @@
     per_step = (HALF, LANES, CH)
     heads = (HALF, HID, LANES)
     scratch = [
-        (cells, F32), (cells, F32), (per_step, F32), (per_step, F32), (heads, F32), (heads, F32),
+        (cells, F32), (cells, F32), (cells, F32), (per_step, F32), (per_step, F32), (heads, F32), (heads, F32),
         (per_step, BF16),
-        ((HID * HALF, LANES), F32),
+        ((HID * HALF, LANES), F32), ((HID * HALF, LANES), F32),
         (block8, BF16),
         ((2,) + block8, BF16),
         ((COLC, ROW * SIDE, LANES), BF16),
@@ -402,7 +409,7 @@
             pltpu.SemaphoreType.DMA((4,)),
             pltpu.SemaphoreType.DMA((4,)),
             pltpu.SemaphoreType.DMA((8, NCH)),
-            pltpu.SemaphoreType.REGULAR,
+            pltpu.SemaphoreType.DMA,
         ],
         compiler_params=pltpu.CompilerParams(
             collective_id=0, has_side_effects=True, vmem_limit_bytes=58 * 1024 * 1024
@@ -417,6 +424,18 @@
         w_out,
         cotangent,
     )
+    update, grad_pair, grad_right = pl.pallas_call(
+        store,
+        out_shape=(
+            jax.ShapeDtypeStruct(cells, F32),
+            jax.ShapeDtypeStruct(cells, F32),
+            jax.ShapeDtypeStruct((HID, SIDE, KB), BF16),
+        ),
+        in_specs=[vmem, vmem, vmem],
+        out_specs=(any_spec, any_spec, any_spec),
+        scratch_shapes=[pltpu.SemaphoreType.DMA((3,))],
+        compiler_params=pltpu.CompilerParams(vmem_limit_bytes=1024 * 1024),
+    )(*(pltpu.with_memory_space_constraint(a, pltpu.VMEM) for a in (update, grad_pair, grad_right)))
     return update, grad_pair, jnp.transpose(grad_right, (0, 2, 1))
 
 

time: 79.5 us -> 73.4 us (0.923)
  local copies, waits for them, and re-layouts: 3.61 us -> 0 us
  Pallas kernels: 75.1 us -> 72.5 us
    pallas_call x1, Pallas kernels: 75.1 us -> 70.2 us  [shards(): pl.pallas_call(kernel, out_shape=(pltpu.VMEM(cells, F32), pltpu.VMEM(cell...]
    unnamed x3 -> x0, local copies, waits for them, and re-layouts: 3.61 us -> none
    pallas_call x0 -> x1, Pallas kernels: none -> 2.38 us  [shards(): pl.pallas_call(store, out_shape=(jax.ShapeDtypeStruct(cells, F32), jax.Sh...]
where the time goes in v4:
time: 73.4 us; the launch traced here: 73.2 us
  Pallas kernels  72.5 us (99%)
    pallas_call x1, Pallas kernels, shards(): pl.pallas_call(kernel, out_shape=(pltpu.VMEM(cells, F32), pltpu.VMEM(cell...  70.2 us
    pallas_call x1, Pallas kernels, shards(): pl.pallas_call(store, out_shape=(jax.ShapeDtypeStruct(cells, F32), jax.Sh...  2.38 us

profile of v4, /device:TPU:1, one launch (start us, length us, event | category | flops | bytes accessed | tf_op | source)
XLA Modules:
  0.0 73.2 jit_solution(3828741226166870291)
XLA Ops:
  0.6 70.2 %shard_map.103 = (f32[64,64,128]{2,1,0:T(8,128)S(1)}, f32[64,64,128]{2,1,0:T(8,128)S(1)}, bf16[64,64,128]{2,1,0:T(8,128)(2,1)S(1)}) custom-call(f32[64,64,128]{2,1,0:T(8,128)} %pair_hbm.1, bf16[64,64,128]{2,1,0:T(8,128)(2,1)} %bitcast.5, bf16[64,128]{1,0:T(8,128)(2,1)} %bitcast.6, bf16[64,128]{1,0:T(8,128)(2,1)} %bitcast.7, bf16[128,128]{1,0:T(8,128)(2,1)} %wg_ref.1, ...), custom_call_target="tpu_custom_call" | custom-call | tf_op jit(solution)/shard_map/pallas_call | solution.py:401
  70.8 2.4 %shard_map.104 = (f32[64,64,128]{2,1,0:T(8,128)}, f32[64,64,128]{2,1,0:T(8,128)}, bf16[64,64,128]{2,1,0:T(8,128)(2,1)}) custom-call(f32[64,64,128]{2,1,0:T(8,128)S(1)} %get-tuple-element.9.upd, f32[64,64,128]{2,1,0:T(8,128)S(1)} %get-tuple-element.10.gp, bf16[64,64,128]{2,1,0:T(8,128)(2,1)S(1)} %get-tuple-element.11.gr), custom_call_target="tpu_custom_call" | custom-call | tf_op jit(solution)/shard_map/pallas_call | solution.py:427

commit v5 on v4

--- a/solution.py
+++ b/solution.py
@@ -50,7 +50,7 @@
     pair_hbm, right_hbm, wlg_ref, wl_ref, wg_ref, gain_ref, wo_ref, cot_hbm,
     upd, gp, gr,
     raw, xn, cot, inv, gate, sig, val, dgate,
-    stage, stage_d, send_l, lb, lfull, rt, tm, tr, dts, dtr, dtfull, grs, dlk, dlx, dly, dls, dlr, wcat, gcol,
+    stage, stage_d, send_l, lb, lfull, rt, tm, tr, dts, dtr, dtfull, grsum, grs, dlk, dlx, dly, dls, dlr, wcat, gcol,
     io_sem, send_sem, recv_sem, tri_sem, line_sem,
 ):
     row, col = lax.axis_index("row"), lax.axis_index("col")
@@ -132,23 +132,29 @@
         sig[s] = left_sig
         stage[stage_rows(t, n), :] = left_sig * value
 
-    steps(left_step, 0)
+    def stage_block(t, h):
+        return pl.ds(pl.multiple_of((t * HID + h) * SB, SB), SB)
+
+    def project_left(t):
+        steps(left_step, t)
+
+        def pack_left(h, _):
+            send_l[t, h] = stage[stage_block(t, h), :].astype(BF16)
+            return 0
+
+        lax.fori_loop(0, HID, pack_left, 0, unroll=8)
+
+    def send_left(t):
+        keep(lambda q: send_l.at[t, q], lb.at[t, core, me], tri_sem.at[9, t])
+        exchange(lambda q: send_l.at[t, q], lb.at[t, core, me], tri_sem.at[8, t], tri_sem.at[9, t])
+
+    project_left(0)
     pl.semaphore_wait(barrier, len(NEAR) + 1)
     exchange(lambda q: right_hbm.at[q], rt.at[me], send_sem.at[0], line_sem, LINE)
-    steps(left_step, 1)
-
-    def stage_block(t, h):
-        return pl.ds(pl.multiple_of((t * HID + h) * SB, SB), SB)
-
-    def pack_left(h, _):
-        send_l[h] = jnp.concatenate([stage[stage_block(t, h), :] for t in range(NCH)], axis=0).astype(BF16)
-        return 0
-
-    lax.fori_loop(0, HID, pack_left, 0, unroll=4)
+    keep(lambda q: right_hbm.at[q], rt.at[me], recv_sem.at[0])
+    project_left(1)
     arrived(rt.at[pl.ds(0, len(LINE))], line_sem)
-    keep(lambda q: send_l.at[q], lb.at[core, me], recv_sem.at[1])
-    exchange(lambda q: send_l.at[q], lb.at[core, me], send_sem.at[1], recv_sem.at[1])
-    keep(lambda q: right_hbm.at[q], rt.at[me], recv_sem.at[0])
+    send_left(0)
     exchange(lambda q: right_hbm.at[q], rt.at[me], send_sem.at[0], recv_sem.at[0], REST)
 
     def gate_step(s, _):
@@ -158,28 +164,29 @@
 
     lax.fori_loop(0, HALF, gate_step, 0, unroll=UNROLL)
 
-    arrived(lb.at[core], recv_sem.at[1])
-    swap_left = pltpu.make_async_remote_copy(
-        src_ref=lb.at[core],
-        dst_ref=lb.at[core],
-        send_sem=send_sem.at[2],
-        recv_sem=recv_sem.at[2],
-        device_id=sibling,
-        device_id_type=MESH,
-    )
-    swap_left.start()
-    arrived(lb.at[1 - core], recv_sem.at[2])
-
-    def unpack_left(q, _):
-        r, c = q // COLC, lax.rem(q, COLC)
-        top, bottom = swap(lb[0, q].astype(F32), lb[1, q].astype(F32))
-        for t in range(NCH):
-            block = jnp.concatenate([top[t * SB : (t + 1) * SB], bottom[t * SB : (t + 1) * SB]], axis=0)
-            at = pl.multiple_of(t * TR + r * 2 * SB, 2 * SB)
-            lfull[c, pl.ds(at, 2 * SB), :] = block.astype(BF16)
-        return 0
-
-    lax.fori_loop(0, PEERS, unpack_left, 0, unroll=4)
+    def swap_left(t):
+        return pltpu.make_async_remote_copy(
+            src_ref=lb.at[t, core],
+            dst_ref=lb.at[t, core],
+            send_sem=tri_sem.at[10, t],
+            recv_sem=tri_sem.at[11, t],
+            device_id=sibling,
+            device_id_type=MESH,
+        )
+
+    def take_left(t):
+        arrived(lb.at[t, core], tri_sem.at[9, t])
+        swap_left(t).start()
+        arrived(lb.at[t, 1 - core], tri_sem.at[11, t])
+
+        def unpack_left(q, _):
+            r, c = q // COLC, lax.rem(q, COLC)
+            top, bottom = swap(lb[t, 0, q].astype(F32), lb[t, 1, q].astype(F32))
+            block = jnp.concatenate([top, bottom], axis=0).astype(BF16)
+            lfull[c, pl.ds(pl.multiple_of(t * TR + r * 2 * SB, 2 * SB), 2 * SB), :] = block
+            return 0
+
+        lax.fori_loop(0, PEERS, unpack_left, 0, unroll=8)
 
     def k_left(lo, rows=slice(None)):
         return jnp.concatenate([lfull[lo, rows], lfull[lo + 1, rows]], axis=1)
@@ -189,9 +196,14 @@
         b = jnp.concatenate([rt[(lo + 1) * COLC + c] for c in range(COLC)], axis=0)
         return jnp.concatenate([a, b], axis=1)
 
+    send_left(1)
+    take_left(0)
+    sent(right_hbm, send_sem.at[0])
     arrived(rt.at[pl.ds(0, PEERS - len(LINE))], recv_sem.at[0])
 
     for t in range(NCH):
+        if t:
+            take_left(t)
         rows = slice(t * TR, (t + 1) * TR)
         total = dot(k_left(0, rows), k_right(0), 1, 1)
         for lo in range(2, ROW, 2):
@@ -305,18 +317,29 @@
         keep(lambda q: dls.at[t, q], dlr.at[t, me], tri_sem.at[7, t])
         exchange(lambda q: dls.at[t, q], dlr.at[t, me], tri_sem.at[6, t], tri_sem.at[7, t])
 
+    def right_grad(t):
+        rows = slice(t * TR, (t + 1) * TR)
+        d_tri = jnp.concatenate([dtfull[p, rows] for p in range(COLC // 2)], axis=1)
+        for lo in range(0, COLC, 2):
+            part = dot(d_tri, k_left(lo, rows), 0, 0)
+            if t:
+                part += grsum[lo // 2]
+            if t < NCH - 1:
+                grsum[lo // 2] = part
+                continue
+            part = part.astype(BF16)
+            for c in range(2):
+                for cc in range(COLC):
+                    grs[(lo + c) * COLC + cc] = part[cc * SIDE : (cc + 1) * SIDE, c * LANES : (c + 1) * LANES]
+
     for t in range(NCH - 1):
         tri_grad(t)
         left_grad(t)
+        right_grad(t)
         send_left_grad(t)
     tri_grad(NCH - 1)
 
-    d_tri_all = jnp.concatenate([dtfull[p] for p in range(COLC // 2)], axis=1)
-    for lo in range(0, COLC, 2):
-        part = dot(d_tri_all, k_left(lo), 0, 0).astype(BF16)
-        for c in range(2):
-            for cc in range(COLC):
-                grs[(lo + c) * COLC + cc] = part[cc * SIDE : (cc + 1) * SIDE, c * LANES : (c + 1) * LANES]
+    right_grad(NCH - 1)
 
     def send_right_grad(others):
         exchange(lambda q: grs.at[q], gr.at[me], send_sem.at[3], recv_sem.at[3], others)
@@ -349,12 +372,11 @@
         widen(dlr, t)
         steps(final_step, t)
 
-    sent(right_hbm, send_sem.at[0])
-    sent(send_l, send_sem.at[1])
-    swap_left.wait_send()
     for t in range(NCH):
         sent(dts.at[t], tri_sem.at[2, t])
         swap_grad(t).wait_send()
+        sent(send_l.at[t], tri_sem.at[8, t])
+        swap_left(t).wait_send()
     sent(tm.at[NCH - 1], tri_sem.at[0, NCH - 1])
     for t in range(NCH):
         sent(dls.at[t], tri_sem.at[6, t])
@@ -377,7 +399,6 @@
     any_spec = pl.BlockSpec(memory_space=pl.ANY)
     vmem = pl.BlockSpec(memory_space=pltpu.VMEM)
     cells = (SIDE, SIDE, CH)
-    block8 = (PEERS, HALF, LANES)
     chunks = (NCH, PEERS, SB, LANES)
     block16 = (PEERS, SIDE, KB)
     per_step = (HALF, LANES, CH)
@@ -386,12 +407,13 @@
         (cells, F32), (cells, F32), (cells, F32), (per_step, F32), (per_step, F32), (heads, F32), (heads, F32),
         (per_step, BF16),
         ((HID * HALF, LANES), F32), ((HID * HALF, LANES), F32),
-        (block8, BF16),
-        ((2,) + block8, BF16),
+        (chunks, BF16),
+        ((NCH, 2, PEERS, SB, LANES), BF16),
         ((COLC, ROW * SIDE, LANES), BF16),
         (block16, BF16),
         (chunks, BF16), (chunks, BF16), (chunks, BF16), (chunks, BF16),
         ((COLC // 2, ROW * SIDE, LANES), BF16),
+        ((COLC // 2, COLC * SIDE, 2 * LANES), F32),
         (block16, BF16),
         (chunks, F32),
         (chunks, BF16), (chunks, BF16), (chunks, BF16), (chunks, BF16),
@@ -408,7 +430,7 @@
             pltpu.SemaphoreType.DMA((2,)),
             pltpu.SemaphoreType.DMA((4,)),
             pltpu.SemaphoreType.DMA((4,)),
-            pltpu.SemaphoreType.DMA((8, NCH)),
+            pltpu.SemaphoreType.DMA((12, NCH)),
             pltpu.SemaphoreType.DMA,
         ],
         compiler_params=pltpu.CompilerParams(

time: 73.4 us -> 72.1 us (0.982)
  Pallas kernels: 72.5 us -> 71.3 us
    pallas_call x1, Pallas kernels: 70.2 us -> 68.9 us  [shards(): pl.pallas_call(kernel, out_shape=(pltpu.VMEM(cells, F32), pltpu.VMEM(cell...]
where the time goes in v5:
time: 72.1 us; the launch traced here: 71.9 us
  Pallas kernels  71.3 us (99%)
    pallas_call x1, Pallas kernels, shards(): pl.pallas_call(kernel, out_shape=(pltpu.VMEM(cells, F32), pltpu.VMEM(cell...  68.9 us
    pallas_call x1, Pallas kernels, shards(): pl.pallas_call(store, out_shape=(jax.ShapeDtypeStruct(cells, F32), jax.Sh...  2.38 us

profile of v5, /device:TPU:1, one launch (start us, length us, event | category | flops | bytes accessed | tf_op | source)
XLA Modules:
  0.0 71.9 jit_solution(8890670821430112155)
XLA Ops:
  0.6 68.9 %shard_map.103 = (f32[64,64,128]{2,1,0:T(8,128)S(1)}, f32[64,64,128]{2,1,0:T(8,128)S(1)}, bf16[64,64,128]{2,1,0:T(8,128)(2,1)S(1)}) custom-call(f32[64,64,128]{2,1,0:T(8,128)} %pair_hbm.1, bf16[64,64,128]{2,1,0:T(8,128)(2,1)} %bitcast.5, bf16[64,128]{1,0:T(8,128)(2,1)} %bitcast.6, bf16[64,128]{1,0:T(8,128)(2,1)} %bitcast.7, bf16[128,128]{1,0:T(8,128)(2,1)} %wg_ref.1, ...), custom_call_target="tpu_custom_call" | custom-call | tf_op jit(solution)/shard_map/pallas_call | solution.py:423
  69.6 2.4 %shard_map.104 = (f32[64,64,128]{2,1,0:T(8,128)}, f32[64,64,128]{2,1,0:T(8,128)}, bf16[64,64,128]{2,1,0:T(8,128)(2,1)}) custom-call(f32[64,64,128]{2,1,0:T(8,128)S(1)} %get-tuple-element.9.upd, f32[64,64,128]{2,1,0:T(8,128)S(1)} %get-tuple-element.10.gp, bf16[64,64,128]{2,1,0:T(8,128)(2,1)S(1)} %get-tuple-element.11.gr), custom_call_target="tpu_custom_call" | custom-call | tf_op jit(solution)/shard_map/pallas_call | solution.py:449

commit v6 on v5

--- a/solution.py
+++ b/solution.py
@@ -217,8 +217,6 @@
                 )
                 tm[t, r * COLC + 2 * p] = a.astype(BF16)
                 tm[t, r * COLC + 2 * p + 1] = b.astype(BF16)
-        if t:
-            sent(tm.at[t - 1], tri_sem.at[0, t - 1])
         keep(lambda q: tm.at[t, q], tr.at[t, me], tri_sem.at[1, t])
         exchange(lambda q: tm.at[t, q], tr.at[t, me], tri_sem.at[0, t], tri_sem.at[1, t])
 
@@ -377,7 +375,8 @@
         swap_grad(t).wait_send()
         sent(send_l.at[t], tri_sem.at[8, t])
         swap_left(t).wait_send()
-    sent(tm.at[NCH - 1], tri_sem.at[0, NCH - 1])
+    for t in range(NCH):
+        sent(tm.at[t], tri_sem.at[0, t])
     for t in range(NCH):
         sent(dls.at[t], tri_sem.at[6, t])
     sent(grs, send_sem.at[3])

time: 72.1 us -> 72.1 us (level)
  no operation moved by 1% of the time
where the time goes in v6:
time: 72.1 us; the launch traced here: 71.9 us
  Pallas kernels  71.3 us (99%)
    pallas_call x1, Pallas kernels, shards(): pl.pallas_call(kernel, out_shape=(pltpu.VMEM(cells, F32), pltpu.VMEM(cell...  68.9 us
    pallas_call x1, Pallas kernels, shards(): pl.pallas_call(store, out_shape=(jax.ShapeDtypeStruct(cells, F32), jax.Sh...  2.38 us

profile of v6, /device:TPU:1, one launch (start us, length us, event | category | flops | bytes accessed | tf_op | source)
XLA Modules:
  0.0 71.9 jit_solution(3038976609188295057)
XLA Ops:
  0.6 68.9 %shard_map.103 = (f32[64,64,128]{2,1,0:T(8,128)S(1)}, f32[64,64,128]{2,1,0:T(8,128)S(1)}, bf16[64,64,128]{2,1,0:T(8,128)(2,1)S(1)}) custom-call(f32[64,64,128]{2,1,0:T(8,128)} %pair_hbm.1, bf16[64,64,128]{2,1,0:T(8,128)(2,1)} %bitcast.5, bf16[64,128]{1,0:T(8,128)(2,1)} %bitcast.6, bf16[64,128]{1,0:T(8,128)(2,1)} %bitcast.7, bf16[128,128]{1,0:T(8,128)(2,1)} %wg_ref.1, ...), custom_call_target="tpu_custom_call" | custom-call | tf_op jit(solution)/shard_map/pallas_call | solution.py:422
  69.6 2.4 %shard_map.104 = (f32[64,64,128]{2,1,0:T(8,128)}, f32[64,64,128]{2,1,0:T(8,128)}, bf16[64,64,128]{2,1,0:T(8,128)(2,1)}) custom-call(f32[64,64,128]{2,1,0:T(8,128)S(1)} %get-tuple-element.9.upd, f32[64,64,128]{2,1,0:T(8,128)S(1)} %get-tuple-element.10.gp, bf16[64,64,128]{2,1,0:T(8,128)(2,1)S(1)} %get-tuple-element.11.gr), custom_call_target="tpu_custom_call" | custom-call | tf_op jit(solution)/shard_map/pallas_call | solution.py:448

commit v7 on v5

--- a/solution.py
+++ b/solution.py
@@ -345,10 +345,10 @@
         exchange(lambda q: grs.at[q], gr.at[me], send_sem.at[3], recv_sem.at[3], others)
 
     keep(lambda q: grs.at[q], gr.at[me], recv_sem.at[3])
-    send_right_grad(OTHERS[0::4])
+    send_right_grad(OTHERS[0::8])
     left_grad(NCH - 1)
     send_left_grad(NCH - 1)
-    send_right_grad([v for n, v in enumerate(OTHERS) if n % 4])
+    send_right_grad([v for n, v in enumerate(OTHERS) if n % 8])
 
     def final_step(t, n):
         s = t * SB + n

time: 72.1 us -> 72.5 us (level)
  no operation moved by 1% of the time
where the time goes in v7:
time: 72.5 us; the launch traced here: 72.3 us
  Pallas kernels  71.7 us (99%)
    pallas_call x1, Pallas kernels, shards(): pl.pallas_call(kernel, out_shape=(pltpu.VMEM(cells, F32), pltpu.VMEM(cell...  69.3 us
    pallas_call x1, Pallas kernels, shards(): pl.pallas_call(store, out_shape=(jax.ShapeDtypeStruct(cells, F32), jax.Sh...  2.38 us

profile of v7, /device:TPU:1, one launch (start us, length us, event | category | flops | bytes accessed | tf_op | source)
XLA Modules:
  0.0 72.3 jit_solution(8657157631573767372)
XLA Ops:
  0.6 69.3 %shard_map.103 = (f32[64,64,128]{2,1,0:T(8,128)S(1)}, f32[64,64,128]{2,1,0:T(8,128)S(1)}, bf16[64,64,128]{2,1,0:T(8,128)(2,1)S(1)}) custom-call(f32[64,64,128]{2,1,0:T(8,128)} %pair_hbm.1, bf16[64,64,128]{2,1,0:T(8,128)(2,1)} %bitcast.5, bf16[64,128]{1,0:T(8,128)(2,1)} %bitcast.6, bf16[64,128]{1,0:T(8,128)(2,1)} %bitcast.7, bf16[128,128]{1,0:T(8,128)(2,1)} %wg_ref.1, ...), custom_call_target="tpu_custom_call" | custom-call | tf_op jit(solution)/shard_map/pallas_call | solution.py:423
  69.9 2.4 %shard_map.104 = (f32[64,64,128]{2,1,0:T(8,128)}, f32[64,64,128]{2,1,0:T(8,128)}, bf16[64,64,128]{2,1,0:T(8,128)(2,1)}) custom-call(f32[64,64,128]{2,1,0:T(8,128)S(1)} %get-tuple-element.9.upd, f32[64,64,128]{2,1,0:T(8,128)S(1)} %get-tuple-element.10.gp, bf16[64,64,128]{2,1,0:T(8,128)(2,1)S(1)} %get-tuple-element.11.gr), custom_call_target="tpu_custom_call" | custom-call | tf_op jit(solution)/shard_map/pallas_call | solution.py:449
